TPU v7x, 128 devices: a whole 4x4x4 slice. The times are simulated.
128 devices in a mesh: row: 16 (over y_lo, x, core), col: 8 (over z, y_hi).
Axes of the slice: x: 4, y: 4 (y_hi: 2, y_lo: 2; y = y_hi * 2 + y_lo), z: 4, core: 2. Of those that a mesh axis runs over, the one named last changes fastest.
Arguments:
- integrals: bfloat16 [65536, 2048], P(('row', 'col')), may hold values from -6 to 6
- occupied: bfloat16 [256, 256], replicated, may hold values from -0.375 to 0.375
- virtual: bfloat16 [256, 256], replicated, may hold values from -0.375 to 0.375
- pair_mask: int32 [16, 32], replicated, may hold values 0 or 1
- green_mask: int32 [2, 4, 4], replicated, may hold values 0 or 1
Outputs:
- polarizability: float32 [2048, 2048], P(('row', 'col'))
All inputs are finite; a program needn't handle non-finite values.
Results may differ from a plain program's by a relative error of at most 0.0041.
Values may be sent and summed in bfloat16 or wider, within the bound.
A program may use at most 64 MiB of HBM per device.

v0:
```python
import jax
import jax.numpy as jnp
from jax import lax
from jax.sharding import PartitionSpec as P


def expand_green(green, green_gate):
    blocks = green_gate.shape[0]
    orbitals = green.shape[0]
    width = orbitals // blocks
    scaled = (
        green.reshape(blocks, width, blocks, width)
        * green_gate.astype(jnp.bfloat16)[:, None, :, None]
    )
    return scaled.reshape(orbitals, orbitals)


def local(integrals, occupied, virtual, pair_mask, green_mask):
    orbitals = occupied.shape[0]
    ri_total = integrals.shape[1]
    mu_local = integrals.shape[0] // orbitals
    n_col = lax.axis_size("col")
    blk_count = green_mask.shape[1]
    width = orbitals // blk_count
    ri_blocks = pair_mask.shape[1]
    first_mu = (lax.axis_index("row") * n_col + lax.axis_index("col")) * mu_local
    mu_blocks = (first_mu + jnp.arange(mu_local, dtype=jnp.int32)) // width
    onehot = (mu_blocks[:, None] == jnp.arange(blk_count, dtype=jnp.int32)[None, :]).astype(
        jnp.float32
    )
    selected = jnp.einsum(
        "mb,bnq->mnq",
        onehot,
        pair_mask.reshape(blk_count, blk_count, ri_blocks).astype(jnp.float32),
    ).astype(jnp.bfloat16)
    masked = (
        integrals.reshape(mu_local, blk_count, width, ri_blocks, width)
        * selected[:, :, None, :, None]
    ).reshape(mu_local * orbitals, ri_total)
    occ_masked = expand_green(occupied, green_mask[0])
    virt_masked = expand_green(virtual, green_mask[1])
    half_done = jnp.einsum(
        "mnp,ns->pms",
        masked.reshape(mu_local, orbitals, ri_total),
        virt_masked,
        preferred_element_type=jnp.float32,
    ).astype(jnp.bfloat16)
    by_ri = lax.all_to_all(half_done, ("row", "col"), split_axis=0, concat_axis=1, tiled=True)
    both_done = jnp.einsum(
        "lm,pms->pls", occ_masked, by_ri, preferred_element_type=jnp.float32
    ).astype(jnp.bfloat16)
    returned = lax.all_to_all(both_done, ("row", "col"), split_axis=1, concat_axis=0, tiled=True)
    flat_pairs = returned.reshape(ri_total, mu_local * orbitals)
    summed = lax.psum_scatter(
        jnp.dot(flat_pairs, masked, preferred_element_type=jnp.float32),
        ("row", "col"),
        scatter_dimension=0,
        tiled=True,
    )
    return summed / orbitals


def solution(mesh):
    return jax.shard_map(
        local,
        mesh=mesh,
        in_specs=(P(("row", "col"), None), P(), P(), P(), P()),
        out_specs=P(("row", "col"), None),
        check_vma=False,
    )
```

profile of v0, /device:TPU:0, one launch (start us, length us, event | category | flops | bytes accessed | tf_op | source)
XLA Modules:
  0.0 802.2 jit_solution(16940489898267320050)
XLA Ops:
  6.5 0.7 convert.4
  7.2 0.7 convert_element_type.39
  7.9 0.2 convolution_convert_fusion.1
  8.1 0.1 mul.44
  8.3 0.2 mul.45
  8.5 2.6 mul.49
  11.1 0.0 copy-start.2
  11.1 5.8 mul.50
  16.9 0.0 copy-done.2
  16.9 3.7 fusion
  20.6 6.2 copy.21
  26.7 11.1 %all-to-all-start = ((bf16[2048,2,256]{2,1,0:T(2,128)(2,1)}), bf16[2048,2,256]{2,1,0:T(2,128)(2,1)S(1)}, u32[]{:S(2)}, u32[]{:S(2)}) async-start(bf16[2048,2,256]{2,1,0:T(2,128)(2,1)} %copy.21), calls=%async_computation | async-start | bytes 4194304 | tf_op jit(solution)/shard_map/all_to_all | solution.py:48
  37.9 0.1 mul.52
  38.0 0.2 mul.53
  38.2 28.4 %all-to-all-done = bf16[2048,2,256]{2,1,0:T(2,128)(2,1)S(1)} async-done(((bf16[2048,2,256]{2,1,0:T(2,128)(2,1)}), bf16[2048,2,256]{2,1,0:T(2,128)(2,1)S(1)}, u32[]{:S(2)}, u32[]{:S(2)}) %all-to-all-start) | async-done | bytes 2097184 | tf_op jit(solution)/shard_map/all_to_all | solution.py:48
  66.6 0.3 copy.22
  66.9 0.0 copy-start.3
  66.9 0.3 copy.23
  67.2 0.6 copy-done.3
  67.8 1.7 convert_bitcast_fusion
  69.5 3.2 copy.25
  72.7 5.7 all-to-all-start.1
  78.3 0.2 reduce-scatter.2.cloned.1.call-start
  78.6 6.8 mul.55
  85.4 21.7 %all-to-all-done.1 = bf16[16,256,256]{2,0,1:T(8,128)(2,1)S(1)} async-done(((bf16[16,256,256]{2,0,1:T(8,128)(2,1)}), bf16[16,256,256]{2,0,1:T(8,128)(2,1)S(1)}, u32[]{:S(2)}, u32[]{:S(2)}) %all-to-all-start.1) | async-done | bytes 2097184 | tf_op jit(solution)/shard_map/all_to_all | solution.py:52
  107.1 2.4 copy.26
  109.5 0.0 copy-start
  109.5 0.0 copy-start.1
  109.5 0.5 copy.29
  110.0 1.0 copy-done
  111.1 0.6 copy-done.1
  111.7 8.0 %fusion.3 = f32[2048,2048]{1,0:T(8,128)} fusion(bf16[2048,512]{1,0:T(8,128)(2,1)S(1)} %bitcast.39, bf16[512,2048]{1,0:T(8,128)(2,1)S(1)} %copy-done, bf16[512,2048]{1,0:T(8,128)(2,1)S(1)} %copy-done.1), kind=kOutput, calls=%fused_computation.4 | convolution fusion | flops 4296015872 | bytes 23068672 | tf_op jit(solution)/shard_map/dot_general | solution.py:55
  119.7 0.0 reduce-scatter.2.cloned.1.call-update
  119.8 674.0 %reduce-scatter.2.cloned.1.call-done = f32[16,2048]{1,0:T(8,128)} async-done(((f32[2048,2048]{1,0:T(8,128)}), f32[16,2048]{1,0:T(8,128)}) %reduce-scatter.2.cloned.1.call-update) | async-done | bytes 131088 | tf_op jit(solution)/shard_map/reduce_scatter | solution.py:54
  793.7 1.6 broadcast_multiply_fusion
  (3 shorter events, 0.0 us)
Async XLA Ops:
  11.1 5.8 copy-start.2
  26.7 39.9 %all-to-all-start = ((bf16[2048,2,256]{2,1,0:T(2,128)(2,1)}), bf16[2048,2,256]{2,1,0:T(2,128)(2,1)S(1)}, u32[]{:S(2)}, u32[]{:S(2)}) async-start(bf16[2048,2,256]{2,1,0:T(2,128)(2,1)} %copy.21), calls=%async_computation | async-start | bytes 4194304 | tf_op jit(solution)/shard_map/all_to_all | solution.py:48
  66.9 0.9 copy-start.3
  72.7 34.4 %all-to-all-start.1 = ((bf16[16,256,256]{2,0,1:T(8,128)(2,1)}), bf16[16,256,256]{2,0,1:T(8,128)(2,1)S(1)}, u32[]{:S(2)}, u32[]{:S(2)}) async-start(bf16[16,256,256]{2,0,1:T(8,128)(2,1)} %copy.25), calls=%async_computation.1 | async-start | bytes 4194304 | tf_op jit(solution)/shard_map/all_to_all | solution.py:52
  78.3 715.4 %reduce-scatter.2.cloned.1.call-start = ((), (), s32[]{:S(2)}) async-start(), calls=%async_computation.3 | async-start | bytes 16908288 | tf_op jit(solution)/shard_map/reduce_scatter | solution.py:54
  109.5 1.6 copy-start
  109.5 2.2 copy-start.1
Sparse Core Ops, SparseCore 0:
  119.9 673.8 reduce-scatter.1
where the time goes:
time: 803 us; the launch traced here: 802 us
  waiting for transfers between devices  724 us (90%)
  local copies, waits for them, and re-layouts  31 us (4%)
  starting transfers between devices  17 us (2%)
  matrix products  13.6 us (2%)
  between operations  13.5 us (2%)
    reduce_scatter x1, waiting for transfers between devices, local(): lax.psum_scatter(jnp.dot(flat_pairs, masked, preferred_element_type=jnp.f...  674 us
    all_to_all x1, waiting for transfers between devices, local(): lax.all_to_all(half_done, ('row', 'col'), split_axis=0, concat_axis=1, ti...  28.4 us
    all_to_all x1, waiting for transfers between devices, local(): lax.all_to_all(both_done, ('row', 'col'), split_axis=1, concat_axis=0, ti...  21.7 us
  transfers between devices with their start and end apart: 3, of which 3 were waited for; matrix products, arithmetic and copies ran while one was open for 1% of the time, Pallas kernels for 0%

commit v1 on v0

v1 whole, which is shorter than its diff:
```python
import functools

import jax
import jax.numpy as jnp
from jax import lax
from jax.experimental import pallas as pl
from jax.experimental.pallas import tpu as pltpu
from jax.sharding import PartitionSpec as P

F32 = jnp.float32
BF16 = jnp.bfloat16
MESH = pl.DeviceIdType.MESH
CW = 512
QW = 256
NU = 8
DIMS = ("ylo", "x", "z", "yhi")
SIZE = {"ylo": 2, "x": 4, "z": 4, "yhi": 2}
ORDERS = (("x", "y", "z"), ("y", "z", "x"), ("z", "x", "y"))


def parts_of(axis):
    return ("ylo", "yhi") if axis == "y" else (axis,)


def left_after(dims, axis):
    return tuple(d for d in dims if d not in parts_of(axis))


def pick(dims, axis, k):
    at = {"x": k, "z": k} if axis != "y" else {"ylo": k % 2, "yhi": k // 2}
    return tuple(at[d] if d in parts_of(axis) else slice(None) for d in dims)


def shape_of(dims):
    return tuple(SIZE[d] for d in dims)


def device(pos, core):
    return ((pos["y"] % 2) * 8 + pos["x"] * 2 + core, pos["z"] * 2 + pos["y"] // 2)


def iota(shape, axis):
    return lax.broadcasted_iota(jnp.int32, shape, axis)


def kernel(
    ints, occ, virt, pair_gate, green_gate, out,
    mx, gate, vt, perm, hd, hsend, msend, hrecv, mall, spread, occ_t, wide, both_t,
    send_a, recv_a, recv_c, *rest,
):
    acc_a, acc_b, recv_b = rest[:NU], rest[NU : 2 * NU], rest[2 * NU : 3 * NU]
    x_own, x_send, x_recv, h_send, h_recv, m_send, m_recv, p_send, p_recv, r_send, r_recv = rest[3 * NU :]
    row, col = lax.axis_index("row"), lax.axis_index("col")
    core = row % 2
    me = {"x": (row // 2) % 4, "y": (col % 2) * 2 + row // 8, "z": col // 2}
    chip = (row // 2) * 8 + col
    partner = (row - core + (1 - core), col)

    def other(i):
        pos = {
            "x": (me["x"] + i) % 4,
            "y": (me["y"] + i + i // 4) % 4,
            "z": (me["z"] + i + i // 16) % 4,
        }
        return pos

    def chip_of(pos):
        return ((pos["y"] % 2) * 4 + pos["x"]) * 8 + pos["z"] * 2 + pos["y"] // 2

    barrier = pltpu.get_barrier_semaphore()
    pl.semaphore_signal(barrier, inc=1, device_id=partner, device_id_type=MESH)

    @pl.loop(1, 64)
    def _(i):
        pl.semaphore_signal(barrier, inc=1, device_id=device(other(i), core), device_id_type=MESH)

    def tile(t, c):
        return pl.ds(pl.multiple_of((2 * t + c) * 128, 128), 128)

    own = []
    for ch in range(2):
        for t in range(4):
            cp = pltpu.make_async_copy(
                ints.at[:, :, tile(4 * ch + t, core)],
                mx.at[pl.ds(2 * core, 2), :, pl.ds(ch * CW + t * 128, 128)],
                x_own.at[ch, t],
            )
            cp.start()
            own.append(cp)

    lane = iota((1, 128), 1)
    for g in range(4):
        for t in range(8):
            a = pair_gate[(row // 4) * 4 + g, 4 * t + 2 * core].astype(F32)
            b = pair_gate[(row // 4) * 4 + g, 4 * t + 2 * core + 1].astype(F32)
            gate[g : g + 1, t * 128 : (t + 1) * 128] = jnp.where(lane < 64, a, b)
    lane = iota((1, 256), 1)

    def gated(ref, which):
        blocks = []
        for a in range(4):
            line = jnp.zeros((1, 256), F32)
            for b in range(4):
                line = jnp.where(lane // 64 == b, green_gate[which, a, b].astype(F32), line)
            blocks.append(ref[64 * a : 64 * a + 64, :].astype(F32) * line)
        return jnp.concatenate(blocks, axis=0)

    vt[...] = gated(virt, 1).T.astype(BF16)
    r, c = iota((256, 256), 0), iota((256, 256), 1)
    perm[...] = (c == ((r // 4) % 4) * 64 + (r // 16) * 4 + r % 4).astype(F32).astype(BF16)

    pl.semaphore_wait(barrier, 64)
    theirs = []
    for ch in range(2):
        for t in range(4):
            cp = pltpu.make_async_remote_copy(
                src_ref=ints.at[:, :, tile(4 * ch + t, 1 - core)],
                dst_ref=mx.at[pl.ds(2 * core, 2), :, pl.ds(ch * CW + t * 128, 128)],
                send_sem=x_send.at[ch, t],
                recv_sem=x_recv.at[ch, t],
                device_id=partner,
                device_id_type=MESH,
            )
            cp.start()
            theirs.append(cp)

    def send_all(src, dst, send_sem, recv_sem):
        @pl.loop(1, 64)
        def _(i):
            pos = other(i)
            pltpu.make_async_remote_copy(
                src_ref=src.at[chip_of(pos)],
                dst_ref=dst.at[chip],
                send_sem=send_sem,
                recv_sem=recv_sem,
                device_id=device(pos, core),
                device_id_type=MESH,
            ).start()

        dst[chip] = src[chip]

    def wait_all(ref, sem):
        pltpu.make_async_copy(ref.at[pl.ds(0, 63)], ref.at[pl.ds(0, 63)], sem).wait()

    for ch in range(2):
        for t in range(4):
            own[4 * ch + t].wait()
            theirs[4 * ch + t].wait_recv()
        for piece in range(CW // QW):
            lanes = pl.ds(ch * CW + piece * QW, QW)
            part = pl.ds(piece * QW, QW)

            @pl.loop(0, 4)
            def _(k):
                for g in range(4):
                    rows = pl.ds(64 * g, 64)
                    mx[k, rows, lanes] = (mx[k, rows, lanes].astype(F32) * gate[g : g + 1, lanes]).astype(BF16)
                hd[k, :, part] = jnp.dot(vt[...], mx[k, :, lanes], preferred_element_type=F32).astype(BF16)

            for g in range(4):
                rows = pl.ds(64 * g, 64)
                got = jnp.dot(perm[...], hd[:, rows, part].reshape(256, QW), preferred_element_type=F32)
                hsend[ch, pl.ds(16 * g, 16), :, part] = got.astype(BF16).reshape(16, 16, QW)
        send_all(hsend.at[ch], hrecv.at[ch], h_send.at[ch], h_recv.at[ch])
    for ch in range(2):
        for piece in range(CW // QW):
            lanes = pl.ds(ch * CW + piece * QW, QW)
            part = pl.ds(piece * QW, QW)
            for g in range(4):
                rows = pl.ds(64 * g, 64)
                got = jnp.dot(perm[...], mx[:, rows, lanes].reshape(256, QW), preferred_element_type=F32)
                msend[ch, pl.ds(16 * g, 16), :, part] = got.astype(BF16).reshape(16, 16, QW)
        send_all(msend.at[ch], mall.at[0, ch], m_send.at[ch], m_recv.at[ch])

    rr, cc = iota((1024, 256), 0), iota((1024, 256), 1)
    spread[...] = (
        cc == 32 * (rr // 128) + 16 * ((rr // 8) % 2) + 2 * ((rr // 16) % 8) + (rr // 4) % 2
    ).astype(F32).astype(BF16)
    occ_t[...] = gated(occ, 0).astype(BF16)

    @pl.loop(0, 4)
    def _(k):
        rows = pl.ds(pl.multiple_of(k * 256, 256), 256)
        t1 = jnp.dot(spread[rows, :], occ_t[...], preferred_element_type=F32).astype(BF16)
        for n in range(4):
            got = lax.dot_general(
                t1, spread[n * 256 : (n + 1) * 256, :], (((1,), (1,)), ((), ())), preferred_element_type=F32
            )
            wide[rows, n * 256 : (n + 1) * 256] = jnp.where(r % 4 == c % 4, got, 0.0).astype(BF16)

    for ch in range(2):
        wait_all(hrecv.at[ch], h_recv.at[ch])
        for piece in range(CW // QW):
            t = ch * 4 + piece * 2
            for k in range(4):
                rows = pl.ds(k * 256, 256)
                got = jnp.dot(
                    wide[rows, :],
                    hrecv[ch, :, :, pl.ds(piece * QW, QW)].reshape(1024, QW),
                    preferred_element_type=F32,
                )
                both_t[t // 4, pl.ds(t % 4, 2), :, :, :, rows] = got.T.astype(BF16).reshape(2, 4, 2, 16, 256)

    def reach(u, phase, off, src, dst):
        axis = ORDERS[u % 3][phase]
        pos = dict(me)
        pos[axis] = (me[axis] + off) % 4
        return pltpu.make_async_remote_copy(
            src_ref=src,
            dst_ref=dst,
            send_sem=r_send.at[u, phase, off - 1],
            recv_sem=r_recv.at[u, phase, off - 1],
            device_id=device(pos, core),
            device_id_type=MESH,
        )

    sent = []

    def group(u):
        return (0, 1, 0, 1)[u // 2], u // 4, u % 2

    def copies(u, phase):
        order = ORDERS[u % 3]
        d1 = left_after(DIMS, order[0])
        d2 = left_after(d1, order[1])
        res = []
        for off in (2, 1, 3):
            axis = order[phase]
            k = (me[axis] + off) % 4
            if phase == 0:
                src, dst = send_a.at[u, off - 1], recv_a.at[u, off - 1]
            elif phase == 1:
                src, dst = acc_a[u].at[pick(d1, axis, k)], recv_b[u].at[off - 1]
            else:
                src, dst = acc_b[u].at[pick(d2, axis, k)], recv_c.at[u, off - 1]
            res.append((off, k, reach(u, phase, off, src, dst)))
        return res

    def phase_a(u):
        whose, ch, piece = group(u)
        axis = ORDERS[u % 3][0]
        right = mall[whose, ch, :, :, pl.ds(piece * QW, QW)].reshape(1024, QW)
        for off, k, cp in copies(u, 0):
            left = both_t[pick(DIMS, axis, k)].reshape(256, 1024)
            send_a[u, off - 1] = jnp.dot(left, right, preferred_element_type=F32).astype(BF16)
            cp.start()
            sent.append(cp)
        left = both_t[pick(DIMS, axis, me[axis])].reshape(256, 1024)
        d1 = left_after(DIMS, axis)
        acc_a[u][...] = jnp.dot(left, right, preferred_element_type=F32).reshape(shape_of(d1) + (16, QW))

    def phase_b(u):
        order = ORDERS[u % 3]
        d1 = left_after(DIMS, order[0])
        for _, _, cp in copies(u, 0):
            cp.wait_recv()
        total = acc_a[u][...]
        for off in (1, 2, 3):
            total += recv_a[u, off - 1].astype(F32).reshape(total.shape)
        acc_a[u][...] = total
        for _, _, cp in copies(u, 1):
            cp.start()
            sent.append(cp)

    def phase_c(u):
        order = ORDERS[u % 3]
        d1 = left_after(DIMS, order[0])
        for _, _, cp in copies(u, 1):
            cp.wait_recv()
        total = acc_a[u][pick(d1, order[1], me[order[1]])]
        for off in (1, 2, 3):
            total += recv_b[u][off - 1].reshape(total.shape)
        acc_b[u][...] = total
        for _, _, cp in copies(u, 2):
            cp.start()
            sent.append(cp)

    def finish(u):
        order = ORDERS[u % 3]
        d2 = left_after(left_after(DIMS, order[0]), order[1])
        for _, _, cp in copies(u, 2):
            cp.wait_recv()
        total = acc_b[u][pick(d2, order[2], me[order[2]])]
        for off in (1, 2, 3):
            total += recv_c[u, off - 1]
        total = total * (1.0 / 256.0)
        whose, ch, piece = group(u)
        c_of = core if whose == 0 else 1 - core
        for t in range(2):
            out[:, tile(ch * 4 + piece * 2 + t, c_of)] = total[:, t * 128 : (t + 1) * 128]

    def swap(ch):
        return pltpu.make_async_remote_copy(
            src_ref=mall.at[0, ch],
            dst_ref=mall.at[1, ch],
            send_sem=p_send.at[ch],
            recv_sem=p_recv.at[ch],
            device_id=partner,
            device_id_type=MESH,
        )

    for s in range(NU + 3):
        if s < NU:
            if s % 4 == 0:
                wait_all(mall.at[0, s // 4], m_recv.at[s // 4])
                swap(s // 4).start()
            if s % 4 == 2:
                swap(s // 4).wait_recv()
            phase_a(s)
        if 0 <= s - 1 < NU:
            phase_b(s - 1)
        if 0 <= s - 2 < NU:
            phase_c(s - 2)
        if 0 <= s - 3 < NU:
            finish(s - 3)

    for ch in range(2):
        wait_all(hsend.at[ch], h_send.at[ch])
        wait_all(msend.at[ch], m_send.at[ch])
        swap(ch).wait_send()
    for cp in theirs:
        cp.wait_send()
    for cp in sent:
        cp.wait_send()


def local(integrals, occupied, virtual, pair_mask, green_mask):
    vmem = pltpu.VMEM
    dma = pltpu.SemaphoreType.DMA
    acc_a, acc_b, recv_b = [], [], []
    for u in range(NU):
        d1 = left_after(DIMS, ORDERS[u % 3][0])
        d2 = left_after(d1, ORDERS[u % 3][1])
        acc_a.append(vmem(shape_of(d1) + (16, QW), F32))
        acc_b.append(vmem(shape_of(d2) + (16, QW), F32))
        recv_b.append(vmem((3,) + shape_of(d2) + (16, QW), F32))
    scratch = [
        vmem((4, 256, 1024), BF16),
        vmem((8, 1024), F32),
        vmem((256, 256), BF16),
        vmem((256, 256), BF16),
        vmem((4, 256, CW), BF16),
        vmem((2, 64, 16, CW), BF16),
        vmem((2, 64, 16, CW), BF16),
        vmem((2, 64, 16, CW), BF16),
        vmem((2, 2, 64, 16, CW), BF16),
        vmem((1024, 256), BF16),
        vmem((256, 256), BF16),
        vmem((1024, 1024), BF16),
        vmem((2, 4, 4, 2, 16, 1024), BF16),
        vmem((NU, 3, 256, QW), BF16),
        vmem((NU, 3, 256, QW), BF16),
        vmem((NU, 3, 16, QW), F32),
        *acc_a,
        *acc_b,
        *recv_b,
        dma((2, 4)), dma((2, 4)), dma((2, 4)),
        dma((2,)), dma((2,)), dma((2,)), dma((2,)), dma((2,)), dma((2,)),
        dma((NU, 3, 3)), dma((NU, 3, 3)),
    ]
    return pl.pallas_call(
        kernel,
        out_shape=jax.ShapeDtypeStruct((16, 2048), F32),
        in_specs=[
            pl.BlockSpec(memory_space=pl.ANY),
            pl.BlockSpec(memory_space=pltpu.VMEM),
            pl.BlockSpec(memory_space=pltpu.VMEM),
            pl.BlockSpec(memory_space=pltpu.SMEM),
            pl.BlockSpec(memory_space=pltpu.SMEM),
        ],
        out_specs=pl.BlockSpec(memory_space=pltpu.VMEM),
        scratch_shapes=scratch,
        compiler_params=pltpu.CompilerParams(
            collective_id=0, has_side_effects=True, vmem_limit_bytes=50 * 2**20
        ),
        name="polarizability",
    )(integrals.reshape(2, 256, 2048), occupied, virtual, pair_mask, green_mask)


def solution(mesh):
    return jax.shard_map(
        local,
        mesh=mesh,
        in_specs=(P(("row", "col"), None), P(), P(), P(), P()),
        out_specs=P(("row", "col"), None),
        check_vma=False,
    )
```

time: 803 us -> 126 us (0.16)
  waiting for transfers between devices: 724 us -> 0 us
  Pallas kernels: 0 us -> 121 us
  local copies, waits for them, and re-layouts: 31 us -> 5.44 us
  starting transfers between devices: 17 us -> 0 us
  matrix products: 13.6 us -> 0 us
  between operations: 13.5 us -> 0.01 us
    reduce_scatter x1 -> x0, waiting for transfers between devices: 674 us -> none  [local(): lax.psum_scatter(jnp.dot(flat_pairs, masked, preferred_element_type=jnp.f...]
    pallas_call x0 -> x1, Pallas kernels: none -> 121 us  [local(): pl.pallas_call(kernel, out_shape=jax.ShapeDtypeStruct((16, 2048), F32), i...]
    all_to_all x2 -> x0, waiting for transfers between devices: 50.1 us -> none  [the longest x1 28.4 us: local(): lax.all_to_all(half_done, ('row', 'col'), split_axis=0, concat_axis=1, ti...]
    all_to_all x2 -> x0, starting transfers between devices: 16.8 us -> none  [the longest x1 11.1 us: local(): lax.all_to_all(half_done, ('row', 'col'), split_axis=0, concat_axis=1, ti...]
    mul x7 -> x0, local copies, waits for them, and re-layouts: 15.9 us -> none  [the longest x3 15.2 us: local(): integrals.reshape(mu_local, blk_count, width, ri_blocks, width)]
    dot_general x4 -> x0, matrix products: 13.6 us -> none  [the longest x1 8.04 us: local(): jnp.dot(flat_pairs, masked, preferred_element_type=jnp.float32)]
    convert_element_type x4 -> x0, local copies, waits for them, and re-layouts: 9.35 us -> none  [the longest x1 6.17 us: local(): half_done = jnp.einsum('mnp,ns->pms', masked.reshape(mu_local, orbitals,...]
  transfers between devices with their start and end apart: 3 -> 0, of which waited for: 3 -> 0; matrix products, arithmetic and copies ran while one was open for 1% -> 0% of each run, Pallas kernels for 0% -> 0%
where the time goes in v1:
time: 126 us
  Pallas kernels  121 us (96%)
  local copies, waits for them, and re-layouts  5.44 us (4%)
    pallas_call x1, Pallas kernels, local(): pl.pallas_call(kernel, out_shape=jax.ShapeDtypeStruct((16, 2048), F32), i...  121 us
    unnamed x11, local copies, waits for them, and re-layouts  5.44 us

profile of v1, /device:TPU:0, one launch (start us, length us, event | category | flops | bytes accessed | tf_op | source)
XLA Modules:
  0.0 126.1 jit_solution(15861797525550569012)
XLA Ops:
  0.0 0.0 copy-start
  0.0 1.6 %copy-done = bf16[512,2048]{1,0:T(8,128)(2,1)S(1)} copy-done((bf16[512,2048]{1,0:T(8,128)(2,1)S(1)}, bf16[512,2048]{1,0:T(8,128)(2,1)}, u32[]{:S(2)}) %copy-start) | copy-done | bytes 2097176
  1.6 0.0 copy-start.1
  1.6 0.9 copy-done.1
  2.5 0.0 copy-start.2
  2.5 0.9 copy-done.2
  3.4 0.0 copy-start.3
  3.4 0.7 copy-done.3
  4.1 0.0 copy-start.4
  4.1 0.7 copy-done.4
  4.8 120.6 %polarizability.1 = f32[16,2048]{1,0:T(8,128)S(1)} custom-call(bf16[2,256,2048]{2,1,0:T(8,128)(2,1)S(1)} %bitcast.1, bf16[256,256]{1,0:T(8,128)(2,1)S(1)} %copy-done.1, bf16[256,256]{1,0:T(8,128)(2,1)S(1)} %copy-done.2, s32[16,32]{1,0:T(8,128)S(1)} %copy-done.3, s32[2,4,4]{2,1,0:T(4,128)S(1)} %copy-done.4), custom_call_target="tpu_custom_call" | custom-call | tf_op jit(solution)/shard_map/polarizability/pallas_call | solution.py:361
  125.4 0.7 copy.7
Async XLA Ops:
  0.0 1.6 %copy-start = (bf16[512,2048]{1,0:T(8,128)(2,1)S(1)}, bf16[512,2048]{1,0:T(8,128)(2,1)}, u32[]{:S(2)}) copy-start(bf16[512,2048]{1,0:T(8,128)(2,1)} %param.5) | copy-start | bytes 6291460
  1.6 0.9 copy-start.1
  2.5 0.9 copy-start.2
  3.4 0.7 copy-start.3
  4.1 0.7 copy-start.4

commit v2 on v1

--- a/solution.py
+++ b/solution.py
@@ -13,6 +13,7 @@
 CW = 512
 QW = 256
 NU = 8
+LAGS = (8, 16, 24)
 DIMS = ("ylo", "x", "z", "yhi")
 SIZE = {"ylo": 2, "x": 4, "z": 4, "yhi": 2}
 ORDERS = (("x", "y", "z"), ("y", "z", "x"), ("z", "x", "y"))
@@ -44,12 +45,12 @@
 
 
 def kernel(
-    ints, occ, virt, pair_gate, green_gate, out,
-    mx, gate, vt, perm, hd, hsend, msend, hrecv, mall, spread, occ_t, wide, both_t,
+    ints, occ_in, virt_in, pair_in, green_in, out,
+    occ, virt, pair_gate, green_gate, mx, gate, vt, perm, hd, hsend, msend, hrecv, mall, spread, occ_t, wide, both_t,
     send_a, recv_a, recv_c, *rest,
 ):
     acc_a, acc_b, recv_b = rest[:NU], rest[NU : 2 * NU], rest[2 * NU : 3 * NU]
-    x_own, x_send, x_recv, h_send, h_recv, m_send, m_recv, p_send, p_recv, r_send, r_recv = rest[3 * NU :]
+    x_own, x_send, x_recv, h_send, h_recv, m_send, m_recv, p_send, p_recv, r_send, r_recv, s_in, ready = rest[3 * NU :]
     row, col = lax.axis_index("row"), lax.axis_index("col")
     core = row % 2
     me = {"x": (row // 2) % 4, "y": (col % 2) * 2 + row // 8, "z": col // 2}
@@ -67,12 +68,23 @@
     def chip_of(pos):
         return ((pos["y"] % 2) * 4 + pos["x"]) * 8 + pos["z"] * 2 + pos["y"] // 2
 
+    def along(axis, off):
+        pos = dict(me)
+        pos[axis] = (me[axis] + off) % 4
+        return pos
+
     barrier = pltpu.get_barrier_semaphore()
     pl.semaphore_signal(barrier, inc=1, device_id=partner, device_id_type=MESH)
-
-    @pl.loop(1, 64)
-    def _(i):
-        pl.semaphore_signal(barrier, inc=1, device_id=device(other(i), core), device_id_type=MESH)
+    for axis in ("x", "y", "z"):
+        for off in (1, 2, 3):
+            pl.semaphore_signal(
+                barrier, inc=1, device_id=device(along(axis, off), core), device_id_type=MESH
+            )
+    small = []
+    for n, (src, dst) in enumerate(((pair_in, pair_gate), (green_in, green_gate), (virt_in, virt), (occ_in, occ))):
+        cp = pltpu.make_async_copy(src, dst, s_in.at[n])
+        cp.start()
+        small.append(cp)
 
     def tile(t, c):
         return pl.ds(pl.multiple_of((2 * t + c) * 128, 128), 128)
@@ -88,28 +100,7 @@
             cp.start()
             own.append(cp)
 
-    lane = iota((1, 128), 1)
-    for g in range(4):
-        for t in range(8):
-            a = pair_gate[(row // 4) * 4 + g, 4 * t + 2 * core].astype(F32)
-            b = pair_gate[(row // 4) * 4 + g, 4 * t + 2 * core + 1].astype(F32)
-            gate[g : g + 1, t * 128 : (t + 1) * 128] = jnp.where(lane < 64, a, b)
-    lane = iota((1, 256), 1)
-
-    def gated(ref, which):
-        blocks = []
-        for a in range(4):
-            line = jnp.zeros((1, 256), F32)
-            for b in range(4):
-                line = jnp.where(lane // 64 == b, green_gate[which, a, b].astype(F32), line)
-            blocks.append(ref[64 * a : 64 * a + 64, :].astype(F32) * line)
-        return jnp.concatenate(blocks, axis=0)
-
-    vt[...] = gated(virt, 1).T.astype(BF16)
-    r, c = iota((256, 256), 0), iota((256, 256), 1)
-    perm[...] = (c == ((r // 4) % 4) * 64 + (r // 16) * 4 + r % 4).astype(F32).astype(BF16)
-
-    pl.semaphore_wait(barrier, 64)
+    pl.semaphore_wait(barrier, 10)
     theirs = []
     for ch in range(2):
         for t in range(4):
@@ -123,6 +114,39 @@
             )
             cp.start()
             theirs.append(cp)
+
+    def hop(n, axis):
+        for off in (1, 2, 3):
+            pl.semaphore_signal(
+                ready.at[n], inc=1, device_id=device(along(axis, off), core), device_id_type=MESH
+            )
+
+    hop(0, "y")
+    for cp in small:
+        cp.wait()
+    lane = iota((1, 128), 1)
+    for g in range(4):
+        for t in range(8):
+            a = pair_gate[(row // 4) * 4 + g, 4 * t + 2 * core].astype(F32)
+            b = pair_gate[(row // 4) * 4 + g, 4 * t + 2 * core + 1].astype(F32)
+            gate[g : g + 1, t * 128 : (t + 1) * 128] = jnp.where(lane < 64, a, b)
+    lane = iota((1, 256), 1)
+
+    def gated(ref, which):
+        blocks = []
+        for a in range(4):
+            line = jnp.zeros((1, 256), F32)
+            for b in range(4):
+                line = jnp.where(lane // 64 == b, green_gate[which, a, b].astype(F32), line)
+            blocks.append(ref[64 * a : 64 * a + 64, :].astype(F32) * line)
+        return jnp.concatenate(blocks, axis=0)
+
+    vt[...] = gated(virt, 1).T.astype(BF16)
+    r, c = iota((256, 256), 0), iota((256, 256), 1)
+    perm[...] = (c == ((r // 4) % 4) * 64 + (r // 16) * 4 + r % 4).astype(F32).astype(BF16)
+
+    pl.semaphore_wait(ready.at[0], 3)
+    hop(1, "z")
 
     def send_all(src, dst, send_sem, recv_sem):
         @pl.loop(1, 64)
@@ -161,6 +185,8 @@
                 rows = pl.ds(64 * g, 64)
                 got = jnp.dot(perm[...], hd[:, rows, part].reshape(256, QW), preferred_element_type=F32)
                 hsend[ch, pl.ds(16 * g, 16), :, part] = got.astype(BF16).reshape(16, 16, QW)
+        if ch == 0:
+            pl.semaphore_wait(ready.at[1], 3)
         send_all(hsend.at[ch], hrecv.at[ch], h_send.at[ch], h_recv.at[ch])
     for ch in range(2):
         for piece in range(CW // QW):
@@ -203,8 +229,7 @@
 
     def reach(u, phase, off, src, dst):
         axis = ORDERS[u % 3][phase]
-        pos = dict(me)
-        pos[axis] = (me[axis] + off) % 4
+        pos = along(axis, off)
         return pltpu.make_async_remote_copy(
             src_ref=src,
             dst_ref=dst,
@@ -299,7 +324,7 @@
             device_id_type=MESH,
         )
 
-    for s in range(NU + 3):
+    for s in range(NU + LAGS[2]):
         if s < NU:
             if s % 4 == 0:
                 wait_all(mall.at[0, s // 4], m_recv.at[s // 4])
@@ -307,12 +332,12 @@
             if s % 4 == 2:
                 swap(s // 4).wait_recv()
             phase_a(s)
-        if 0 <= s - 1 < NU:
-            phase_b(s - 1)
-        if 0 <= s - 2 < NU:
-            phase_c(s - 2)
-        if 0 <= s - 3 < NU:
-            finish(s - 3)
+        if 0 <= s - LAGS[0] < NU:
+            phase_b(s - LAGS[0])
+        if 0 <= s - LAGS[1] < NU:
+            phase_c(s - LAGS[1])
+        if 0 <= s - LAGS[2] < NU:
+            finish(s - LAGS[2])
 
     for ch in range(2):
         wait_all(hsend.at[ch], h_send.at[ch])
@@ -335,6 +360,10 @@
         acc_b.append(vmem(shape_of(d2) + (16, QW), F32))
         recv_b.append(vmem((3,) + shape_of(d2) + (16, QW), F32))
     scratch = [
+        vmem((256, 256), BF16),
+        vmem((256, 256), BF16),
+        pltpu.SMEM((16, 32), jnp.int32),
+        pltpu.SMEM((2, 4, 4), jnp.int32),
         vmem((4, 256, 1024), BF16),
         vmem((8, 1024), F32),
         vmem((256, 256), BF16),
@@ -356,22 +385,23 @@
         *recv_b,
         dma((2, 4)), dma((2, 4)), dma((2, 4)),
         dma((2,)), dma((2,)), dma((2,)), dma((2,)), dma((2,)), dma((2,)),
-        dma((NU, 3, 3)), dma((NU, 3, 3)),
+        dma((NU, 3, 3)), dma((NU, 3, 3)), dma((4,)),
+        pltpu.SemaphoreType.REGULAR((2,)),
     ]
     return pl.pallas_call(
         kernel,
         out_shape=jax.ShapeDtypeStruct((16, 2048), F32),
         in_specs=[
-            pl.BlockSpec(memory_space=pl.ANY),
-            pl.BlockSpec(memory_space=pltpu.VMEM),
-            pl.BlockSpec(memory_space=pltpu.VMEM),
-            pl.BlockSpec(memory_space=pltpu.SMEM),
-            pl.BlockSpec(memory_space=pltpu.SMEM),
+            pl.BlockSpec(memory_space=pltpu.HBM),
+            pl.BlockSpec(memory_space=pltpu.HBM),
+            pl.BlockSpec(memory_space=pltpu.HBM),
+            pl.BlockSpec(memory_space=pltpu.HBM),
+            pl.BlockSpec(memory_space=pltpu.HBM),
         ],
         out_specs=pl.BlockSpec(memory_space=pltpu.VMEM),
         scratch_shapes=scratch,
         compiler_params=pltpu.CompilerParams(
-            collective_id=0, has_side_effects=True, vmem_limit_bytes=50 * 2**20
+            collective_id=0, has_side_effects=True, vmem_limit_bytes=61 * 2**20
         ),
         name="polarizability",
     )(integrals.reshape(2, 256, 2048), occupied, virtual, pair_mask, green_mask)

time: 126 us -> 92.8 us (0.74)
  Pallas kernels: 121 us -> 90.6 us
  local copies, waits for them, and re-layouts: 5.44 us -> 1.57 us
    pallas_call x1, Pallas kernels: 121 us -> 90.6 us  [local(): pl.pallas_call(kernel, out_shape=jax.ShapeDtypeStruct((16, 2048), F32), i...]
    unnamed x11 -> x1, local copies, waits for them, and re-layouts: 5.44 us -> 1.57 us
where the time goes in v2:
time: 92.8 us; the launch traced here: 92.2 us
  Pallas kernels  90.6 us (98%)
  local copies, waits for them, and re-layouts  1.57 us (2%)
    pallas_call x1, Pallas kernels, local(): pl.pallas_call(kernel, out_shape=jax.ShapeDtypeStruct((16, 2048), F32), i...  90.6 us

profile of v2, /device:TPU:0, one launch (start us, length us, event | category | flops | bytes accessed | tf_op | source)
XLA Modules:
  0.0 92.2 jit_solution(13792757076200319628)
XLA Ops:
  0.0 90.6 %polarizability.1 = f32[16,2048]{1,0:T(8,128)} custom-call(bf16[2,256,2048]{2,1,0:T(8,128)(2,1)} %bitcast.1, bf16[256,256]{1,0:T(8,128)(2,1)} %occ_in.1, bf16[256,256]{1,0:T(8,128)(2,1)} %virt_in.1, s32[16,32]{1,0:T(8,128)} %pair_in.1, s32[2,4,4]{2,1,0:T(4,128)} %green_in.1), custom_call_target="tpu_custom_call" | custom-call | tf_op jit(solution)/shard_map/polarizability/pallas_call | solution.py:391
  90.6 1.6 %copy.7 = f32[16,2048]{1,0:T(8,128)} copy(f32[16,2048]{1,0:T(8,128)} %polarizability.1) | data formatting | bytes 262144

commit v3 on v0

v3 whole, which is shorter than its diff:
```python
import functools

import jax
import jax.numpy as jnp
from jax import lax
from jax.experimental import pallas as pl
from jax.experimental.pallas import tpu as pltpu
from jax.sharding import PartitionSpec as P

F32 = jnp.float32
BF16 = jnp.bfloat16
MESH = pl.DeviceIdType.MESH
QW = 256
H_CHUNKS = ((0, 512), (512, 512))
M_CHUNKS = ((0, 512), (512, 256), (768, 256))
UNITS = tuple(
    (ch, whose, piece) for ch, (_, w) in enumerate(M_CHUNKS) for whose in range(2) for piece in range(w // QW)
)
NT = 2 * len(UNITS)
DIMS = ("ylo", "x", "z", "yhi")
SIZE = {"ylo": 2, "x": 4, "z": 4, "yhi": 2}
ORDERS = (("x", "y", "z"), ("y", "z", "x"), ("z", "x", "y"))


def parts_of(axis):
    return ("ylo", "yhi") if axis == "y" else (axis,)


def left_after(dims, axis):
    return tuple(d for d in dims if d not in parts_of(axis))


def pick(dims, axis, k):
    at = {"x": k, "z": k} if axis != "y" else {"ylo": k % 2, "yhi": k // 2}
    return tuple(at[d] if d in parts_of(axis) else slice(None) for d in dims)


def shape_of(dims):
    return tuple(SIZE[d] for d in dims)


def device(pos, core):
    return ((pos["y"] % 2) * 8 + pos["x"] * 2 + core, pos["z"] * 2 + pos["y"] // 2)


def iota(shape, axis):
    return lax.broadcasted_iota(jnp.int32, shape, axis)


def order_of(t):
    return ORDERS[t % 3]


def dims_of(t):
    d1 = left_after(DIMS, order_of(t)[0])
    return d1, left_after(d1, order_of(t)[1])


AHEAD = len(M_CHUNKS)
PLAN = (("a", 0, 8), ("b", 0, 8), ("c", 0, 8), ("f", 0, 8))


def kernel(*refs):
    refs = list(refs)

    def take(n):
        got = refs[:n]
        del refs[:n]
        return got

    ints, occ_in, virt_in, pair_in, green_in, out = take(6)
    occ, virt, pair_gate, green_gate = take(4)
    mx, gate, vt, perm, hd, spread, occ_t, wide, both_t, stage = take(10)
    hsend, hrecv = take(len(H_CHUNKS)), take(len(H_CHUNKS))
    msend, mall = take(len(M_CHUNKS)), take(len(M_CHUNKS))
    (send_a,) = take(1)
    recv_a, acc_a, send_b, recv_b, acc_b, send_c, recv_c = (take(NT) for _ in range(7))
    x_own, x_send, x_recv, h_send, h_recv, m_send, m_recv, p_send, p_recv, r_send, r_recv, s_in, ready = refs
    row, col = lax.axis_index("row"), lax.axis_index("col")
    core = row % 2
    me = {"x": (row // 2) % 4, "y": (col % 2) * 2 + row // 8, "z": col // 2}
    chip = (row // 2) * 8 + col
    partner = (row - core + (1 - core), col)

    def along(axis, off):
        pos = dict(me)
        pos[axis] = (me[axis] + off) % 4
        return pos

    def other(i):
        return {
            "x": (me["x"] + i) % 4,
            "y": (me["y"] + i + i // 4) % 4,
            "z": (me["z"] + i + i // 16) % 4,
        }

    def chip_of(pos):
        return ((pos["y"] % 2) * 4 + pos["x"]) * 8 + pos["z"] * 2 + pos["y"] // 2

    barrier = pltpu.get_barrier_semaphore()
    pl.semaphore_signal(barrier, inc=1, device_id=partner, device_id_type=MESH)
    lines = [device(along(axis, off), core) for off in (2, 1, 3) for axis in ("x", "y", "z")]
    for there in lines:
        pl.semaphore_signal(barrier, inc=1, device_id=there, device_id_type=MESH)

    small = []
    for n, (src, dst) in enumerate(((pair_in, pair_gate), (green_in, green_gate), (virt_in, virt), (occ_in, occ))):
        cp = pltpu.make_async_copy(src, dst, s_in.at[n])
        cp.start()
        small.append(cp)

    def tile(t, c):
        return pl.ds(pl.multiple_of((2 * t + c) * 128, 128), 128)

    mine = mx.at[pl.ds(2 * core, 2)]
    for t in range(8):
        pltpu.make_async_copy(ints.at[:, :, tile(t, core)], mine.at[:, :, pl.ds(t * 128, 128)], x_own).start()

    r, c = iota((256, 256), 0), iota((256, 256), 1)
    perm[...] = (c == ((r // 4) % 4) * 64 + (r // 16) * 4 + r % 4).astype(F32).astype(BF16)
    lane = iota((1, 128), 1)
    small[0].wait()
    for g in range(4):
        for t in range(8):
            a = pair_gate[(row // 4) * 4 + g, 4 * t + 2 * core].astype(F32)
            b = pair_gate[(row // 4) * 4 + g, 4 * t + 2 * core + 1].astype(F32)
            gate[g : g + 1, t * 128 : (t + 1) * 128] = jnp.where(lane < 64, a, b)

    def gated(ref, which):
        lane = iota((1, 256), 1)
        blocks = []
        for a in range(4):
            line = jnp.zeros((1, 256), F32)
            for b in range(4):
                line = jnp.where(lane // 64 == b, green_gate[which, a, b].astype(F32), line)
            blocks.append(ref[64 * a : 64 * a + 64, :].astype(F32) * line)
        return jnp.concatenate(blocks, axis=0)

    small[1].wait()
    small[2].wait()
    vt[...] = gated(virt, 1).T.astype(BF16)

    pl.semaphore_wait(barrier, 10)
    for there in lines:
        pl.semaphore_signal(ready.at[0], inc=1, device_id=there, device_id_type=MESH)
    for t in range(8):
        pltpu.make_async_remote_copy(
            src_ref=ints.at[:, :, tile(t, 1 - core)],
            dst_ref=mine.at[:, :, pl.ds(t * 128, 128)],
            send_sem=x_send,
            recv_sem=x_recv.at[t // 2],
            device_id=partner,
            device_id_type=MESH,
        ).start()

    def wait_for(ref, sem):
        pltpu.make_async_copy(ref, ref, sem).wait()

    def half(first, lanes):
        @pl.loop(0, 2)
        def _(n):
            k = first + n
            for g in range(4):
                rows = pl.ds(64 * g, 64)
                mx[k, rows, lanes] = (mx[k, rows, lanes].astype(F32) * gate[g : g + 1, lanes]).astype(BF16)
            hd[k, :, lanes] = jnp.dot(vt[...], mx[k, :, lanes], preferred_element_type=F32).astype(BF16)

    def pieces(start, width):
        return [(start + n, n) for n in range(0, width, QW)]

    def to_chips(src, dst, lanes, part):
        for g in range(4):
            got = jnp.dot(
                perm[...], src[:, pl.ds(64 * g, 64), lanes].reshape(256, QW), preferred_element_type=F32
            )
            dst[pl.ds(16 * g, 16), :, part] = got.astype(BF16).reshape(16, 16, QW)

    def send_all(src, dst, send_sem, recv_sem, only=None):
        @pl.loop(1, 64)
        def _(i):
            pos = other(i)

            def start():
                pltpu.make_async_remote_copy(
                    src_ref=src.at[chip_of(pos)],
                    dst_ref=dst.at[chip],
                    send_sem=send_sem,
                    recv_sem=recv_sem,
                    device_id=device(pos, core),
                    device_id_type=MESH,
                ).start()

            if only is None:
                start()
            else:
                apart = (i % 4) * ((i + i // 4) % 4) * ((i + i // 16) % 4)
                pl.when((apart == 0) if only == 0 else (apart != 0))(start)

    def send_h(n, only=None):
        send_all(hsend[n], hrecv[n], h_send.at[n], h_recv.at[n], only)
        if only != 1:
            hrecv[n][chip] = hsend[n][chip]

    def send_m(n):
        send_all(msend[n], mall[n].at[0], m_send.at[n], m_recv.at[n])
        mall[n][0, chip] = msend[n][chip]

    def wait_all(ref, sem):
        wait_for(ref.at[pl.ds(0, 63)], sem)

    wait_for(mine, x_own)
    for start, _ in pieces(0, 1024):
        half(2 * core, pl.ds(start, QW))

    def make_h(n):
        first, width = H_CHUNKS[n]
        for start, at in pieces(first, width):
            wait_for(mx.at[pl.ds(2 - 2 * core, 2), :, pl.ds(start, QW)], x_recv.at[start // QW])
            half(2 - 2 * core, pl.ds(start, QW))
            to_chips(hd, hsend[n], pl.ds(start, QW), pl.ds(at, QW))

    def make_m(n):
        first, width = M_CHUNKS[n]
        for start, at in pieces(first, width):
            to_chips(mx, msend[n], pl.ds(start, QW), pl.ds(at, QW))

    pl.semaphore_wait(ready.at[0], 9)
    for off in (1, 2, 3):
        there = device(along("z", off), core)
        pl.semaphore_signal(ready.at[1], inc=1, device_id=there, device_id_type=MESH)
    make_h(0)
    send_h(0, 0)
    make_h(1)
    pl.semaphore_wait(ready.at[1], 3)
    send_h(0, 1)
    send_h(1)
    for n in range(2, len(H_CHUNKS)):
        make_h(n)
        send_h(n)
    for n in range(len(M_CHUNKS)):
        make_m(n)
        if n < AHEAD:
            send_m(n)

    rr, cc = iota((1024, 256), 0), iota((1024, 256), 1)
    spread[...] = (
        cc == 32 * (rr // 128) + 16 * ((rr // 8) % 2) + 2 * ((rr // 16) % 8) + (rr // 4) % 2
    ).astype(F32).astype(BF16)
    small[3].wait()
    occ_t[...] = gated(occ, 0).astype(BF16)

    @pl.loop(0, 4)
    def _(k):
        rows = pl.ds(pl.multiple_of(k * 256, 256), 256)
        t1 = jnp.dot(spread[rows, :], occ_t[...], preferred_element_type=F32).astype(BF16)
        for n in range(4):
            got = lax.dot_general(
                t1, spread[n * 256 : (n + 1) * 256, :], (((1,), (1,)), ((), ())), preferred_element_type=F32
            )
            wide[rows, n * 256 : (n + 1) * 256] = jnp.where(r % 4 == c % 4, got, 0.0).astype(BF16)

    for n, (first, width) in enumerate(H_CHUNKS):
        wait_all(hrecv[n], h_recv.at[n])
        if n == len(H_CHUNKS) - 1 and AHEAD < len(M_CHUNKS):
            send_m(AHEAD)
        for start, at in pieces(first, width):
            t = start // 128
            for k in range(4):
                rows = pl.ds(k * 256, 256)
                got = jnp.dot(
                    wide[rows, :], hrecv[n][:, :, pl.ds(at, QW)].reshape(1024, QW), preferred_element_type=F32
                )
                both_t[t // 4, pl.ds(t % 4, 2), :, :, :, rows] = got.T.astype(BF16).reshape(2, 4, 2, 16, 256)

    def copies(t, phase):
        order = order_of(t)
        d1, d2 = dims_of(t)
        axis = order[phase]
        res = []
        for off in (2, 1, 3):
            k = (me[axis] + off) % 4
            if phase == 0:
                src = send_a.at[(t // 2,) + pick(DIMS, axis, k) + (slice(None), pl.ds((t % 2) * 128, 128))]
                dst = recv_a[t].at[off - 1]
            elif phase == 1:
                src, dst = send_b[t].at[pick(d1, axis, k)], recv_b[t].at[off - 1]
            else:
                src, dst = send_c[t].at[pick(d2, axis, k)], recv_c[t].at[off - 1]
            res.append(
                pltpu.make_async_remote_copy(
                    src_ref=src,
                    dst_ref=dst,
                    send_sem=r_send.at[phase],
                    recv_sem=r_recv.at[t, phase],
                    device_id=device(along(axis, off), core),
                    device_id_type=MESH,
                )
            )
        return res

    def launch(t, phase):
        for cp in copies(t, phase):
            cp.start()

    def phase_a(u):
        ch, whose, piece = UNITS[u]
        right = mall[ch][whose, :, :, pl.ds(piece * QW, QW)].reshape(1024, QW)
        for ylo in range(2):
            for x in (0, 2):
                left = both_t[ylo, x : x + 2].reshape(256, 1024)
                got = jnp.dot(left, right, preferred_element_type=F32).reshape(2, 4, 2, 16, QW)
                stage[ylo, x : x + 2] = got
                send_a[u, ylo, x : x + 2] = got.astype(BF16)
        for t in (2 * u, 2 * u + 1):
            launch(t, 0)
            axis = order_of(t)[0]
            acc_a[t][...] = stage[pick(DIMS, axis, me[axis]) + (slice(None), pl.ds((t % 2) * 128, 128))]

    def phase_b(t):
        wait_for(recv_a[t], r_recv.at[t, 0])
        total = acc_a[t][...]
        for off in (1, 2, 3):
            total += recv_a[t][off - 1].astype(F32)
        acc_a[t][...] = total
        send_b[t][...] = total.astype(send_b[t].dtype)
        launch(t, 1)

    def phase_c(t):
        axis = order_of(t)[1]
        wait_for(recv_b[t], r_recv.at[t, 1])
        total = acc_a[t][pick(dims_of(t)[0], axis, me[axis])]
        for off in (1, 2, 3):
            total += recv_b[t][off - 1].astype(F32)
        acc_b[t][...] = total
        send_c[t][...] = total.astype(BF16)
        launch(t, 2)

    def finish(t):
        axis = order_of(t)[2]
        wait_for(recv_c[t], r_recv.at[t, 2])
        total = acc_b[t][pick(dims_of(t)[1], axis, me[axis])]
        for off in (1, 2, 3):
            total += recv_c[t][off - 1].astype(F32)
        ch, whose, piece = UNITS[t // 2]
        at = (M_CHUNKS[ch][0] + piece * QW) // 128 + t % 2
        out[:, tile(at, core if whose == 0 else 1 - core)] = total * (1.0 / 256.0)

    def swap(ch):
        return pltpu.make_async_remote_copy(
            src_ref=mall[ch].at[0],
            dst_ref=mall[ch].at[1],
            send_sem=p_send.at[ch],
            recv_sem=p_recv.at[ch],
            device_id=partner,
            device_id_type=MESH,
        )

    for name, u in [(name, u) for name, first, last in PLAN for u in range(first, last)]:
        if name == "a":
            ch, whose, piece = UNITS[u]
            if piece == 0 and whose == 0:
                wait_all(mall[ch].at[0], m_recv.at[ch])
                if ch + AHEAD + 1 < len(M_CHUNKS):
                    send_m(ch + AHEAD + 1)
                swap(ch).start()
            if piece == 0 and whose == 1:
                swap(ch).wait_recv()
            phase_a(u)
        else:
            for t in (2 * u, 2 * u + 1):
                {"b": phase_b, "c": phase_c, "f": finish}[name](t)

    for n in range(len(H_CHUNKS)):
        wait_all(hsend[n], h_send.at[n])
    for n in range(len(M_CHUNKS)):
        wait_all(msend[n], m_send.at[n])
        swap(n).wait_send()
    wait_for(mine, x_send)
    wait_for(send_a.at[pl.ds(0, NT * 3 // 8)], r_send.at[0])
    wait_for(mx.at[pl.ds(0, 3), pl.ds(0, NT * 8)], r_send.at[1])
    wait_for(mx.at[pl.ds(0, 3), pl.ds(0, NT * 2)], r_send.at[2])


def local(integrals, occupied, virtual, pair_mask, green_mask):
    vmem = pltpu.VMEM
    dma = pltpu.SemaphoreType.DMA
    nh, nm = len(H_CHUNKS), len(M_CHUNKS)
    whole = shape_of(DIMS)
    d1 = [shape_of(dims_of(t)[0]) + (16, 128) for t in range(NT)]
    d2 = [shape_of(dims_of(t)[1]) + (16, 128) for t in range(NT)]
    scratch = [
        vmem((256, 256), BF16),
        vmem((256, 256), BF16),
        pltpu.SMEM((16, 32), jnp.int32),
        pltpu.SMEM((2, 4, 4), jnp.int32),
        vmem((4, 256, 1024), BF16),
        vmem((8, 1024), F32),
        vmem((256, 256), BF16),
        vmem((256, 256), BF16),
        vmem((4, 256, 1024), BF16),
        vmem((1024, 256), BF16),
        vmem((256, 256), BF16),
        vmem((1024, 1024), BF16),
        vmem(whole + (16, 1024), BF16),
        vmem(whole + (16, QW), F32),
        *[vmem((64, 16, w), BF16) for _, w in H_CHUNKS],
        *[vmem((64, 16, w), BF16) for _, w in H_CHUNKS],
        *[vmem((64, 16, w), BF16) for _, w in M_CHUNKS],
        *[vmem((2, 64, 16, w), BF16) for _, w in M_CHUNKS],
        vmem((len(UNITS),) + whole + (16, QW), BF16),
        *[vmem((3,) + s, BF16) for s in d1],
        *[vmem(s, F32) for s in d1],
        *[vmem(s, BF16) for s in d1],
        *[vmem((3,) + s, BF16) for s in d2],
        *[vmem(s, F32) for s in d2],
        *[vmem(s, BF16) for s in d2],
        *[vmem((3, 16, 128), BF16) for _ in d2],
        dma, dma, dma((4,)),
        dma((nh,)), dma((nh,)), dma((nm,)), dma((nm,)), dma((nm,)), dma((nm,)),
        dma((3,)), dma((NT, 3)), dma((4,)),
        pltpu.SemaphoreType.REGULAR((2,)),
    ]
    return pl.pallas_call(
        kernel,
        out_shape=jax.ShapeDtypeStruct((16, 2048), F32),
        in_specs=[pl.BlockSpec(memory_space=pltpu.HBM)] * 5,
        out_specs=pl.BlockSpec(memory_space=pltpu.VMEM),
        scratch_shapes=scratch,
        compiler_params=pltpu.CompilerParams(
            collective_id=0, has_side_effects=True, vmem_limit_bytes=61 * 2**20
        ),
        name="polarizability",
    )(integrals.reshape(2, 256, 2048), occupied, virtual, pair_mask, green_mask)


def solution(mesh):
    return jax.shard_map(
        local,
        mesh=mesh,
        in_specs=(P(("row", "col"), None), P(), P(), P(), P()),
        out_specs=P(("row", "col"), None),
        check_vma=False,
    )
```

time: 803 us -> 86.6 us (0.11)
  waiting for transfers between devices: 724 us -> 0 us
  Pallas kernels: 0 us -> 84.5 us
  local copies, waits for them, and re-layouts: 31 us -> 1.57 us
  starting transfers between devices: 17 us -> 0 us
  matrix products: 13.6 us -> 0 us
  between operations: 13.5 us -> 0.01 us
    reduce_scatter x1 -> x0, waiting for transfers between devices: 674 us -> none  [local(): lax.psum_scatter(jnp.dot(flat_pairs, masked, preferred_element_type=jnp.f...]
    pallas_call x0 -> x1, Pallas kernels: none -> 84.5 us  [local(): pl.pallas_call(kernel, out_shape=jax.ShapeDtypeStruct((16, 2048), F32), i...]
    all_to_all x2 -> x0, waiting for transfers between devices: 50.1 us -> none  [the longest x1 28.4 us: local(): lax.all_to_all(half_done, ('row', 'col'), split_axis=0, concat_axis=1, ti...]
    all_to_all x2 -> x0, starting transfers between devices: 16.8 us -> none  [the longest x1 11.1 us: local(): lax.all_to_all(half_done, ('row', 'col'), split_axis=0, concat_axis=1, ti...]
    mul x7 -> x0, local copies, waits for them, and re-layouts: 15.9 us -> none  [the longest x3 15.2 us: local(): integrals.reshape(mu_local, blk_count, width, ri_blocks, width)]
    dot_general x4 -> x0, matrix products: 13.6 us -> none  [the longest x1 8.04 us: local(): jnp.dot(flat_pairs, masked, preferred_element_type=jnp.float32)]
    convert_element_type x4 -> x0, local copies, waits for them, and re-layouts: 9.35 us -> none  [the longest x1 6.17 us: local(): half_done = jnp.einsum('mnp,ns->pms', masked.reshape(mu_local, orbitals,...]
  transfers between devices with their start and end apart: 3 -> 0, of which waited for: 3 -> 0; matrix products, arithmetic and copies ran while one was open for 1% -> 0% of each run, Pallas kernels for 0% -> 0%
where the time goes in v3:
time: 86.6 us; the launch traced here: 86.1 us
  Pallas kernels  84.5 us (98%)
  local copies, waits for them, and re-layouts  1.57 us (2%)
    pallas_call x1, Pallas kernels, local(): pl.pallas_call(kernel, out_shape=jax.ShapeDtypeStruct((16, 2048), F32), i...  84.5 us

profile of v3, /device:TPU:0, one launch (start us, length us, event | category | flops | bytes accessed | tf_op | source)
XLA Modules:
  0.0 86.1 jit_solution(130284982131483539)
XLA Ops:
  0.0 84.5 %polarizability.1 = f32[16,2048]{1,0:T(8,128)} custom-call(bf16[2,256,2048]{2,1,0:T(8,128)(2,1)} %bitcast.1, bf16[256,256]{1,0:T(8,128)(2,1)} %refs_1_.1, bf16[256,256]{1,0:T(8,128)(2,1)} %refs_2_.1, s32[16,32]{1,0:T(8,128)} %refs_3_.1, s32[2,4,4]{2,1,0:T(4,128)} %refs_4_.1), custom_call_target="tpu_custom_call" | custom-call | tf_op jit(solution)/shard_map/polarizability/pallas_call | solution.py:423
  84.5 1.6 %copy.7 = f32[16,2048]{1,0:T(8,128)} copy(f32[16,2048]{1,0:T(8,128)} %polarizability.1) | data formatting | bytes 262144

commit v4 on v3

--- a/solution.py
+++ b/solution.py
@@ -11,8 +11,8 @@
 BF16 = jnp.bfloat16
 MESH = pl.DeviceIdType.MESH
 QW = 256
-H_CHUNKS = ((0, 512), (512, 512))
-M_CHUNKS = ((0, 512), (512, 256), (768, 256))
+H_CHUNKS = ((0, 256), (256, 256), (512, 512))
+M_CHUNKS = ((0, 256), (256, 256), (512, 512))
 UNITS = tuple(
     (ch, whose, piece) for ch, (_, w) in enumerate(M_CHUNKS) for whose in range(2) for piece in range(w // QW)
 )
@@ -56,8 +56,12 @@
     return d1, left_after(d1, order_of(t)[1])
 
 
+DIRECT = (6, 7)
 AHEAD = len(M_CHUNKS)
 PLAN = (("a", 0, 8), ("b", 0, 8), ("c", 0, 8), ("f", 0, 8))
+
+
+DIRECT_TILES = tuple(2 * u + n for u in DIRECT for n in range(2))
 
 
 def kernel(*refs):
@@ -75,6 +79,7 @@
     msend, mall = take(len(M_CHUNKS)), take(len(M_CHUNKS))
     (send_a,) = take(1)
     recv_a, acc_a, send_b, recv_b, acc_b, send_c, recv_c = (take(NT) for _ in range(7))
+    recv_d = dict(zip(DIRECT_TILES, take(len(DIRECT_TILES))))
     x_own, x_send, x_recv, h_send, h_recv, m_send, m_recv, p_send, p_recv, r_send, r_recv, s_in, ready = refs
     row, col = lax.axis_index("row"), lax.axis_index("col")
     core = row % 2
@@ -290,7 +295,7 @@
                 pltpu.make_async_remote_copy(
                     src_ref=src,
                     dst_ref=dst,
-                    send_sem=r_send.at[phase],
+                    send_sem=r_send.at[min(phase, 1)],
                     recv_sem=r_recv.at[t, phase],
                     device_id=device(along(axis, off), core),
                     device_id_type=MESH,
@@ -301,6 +306,23 @@
     def launch(t, phase):
         for cp in copies(t, phase):
             cp.start()
+
+    def launch_direct(t):
+        _, one, two = order_of(t)
+        d1, d2 = dims_of(t)
+        for n in range(15, 0, -1):
+            pos = along(one, n // 4)
+            pos[two] = (me[two] + n % 4) % 4
+            at = dict(zip(d1, pick(d1, one, pos[one])))
+            at.update(zip(d2, pick(d2, two, pos[two])))
+            pltpu.make_async_remote_copy(
+                src_ref=send_b[t].at[tuple(at[d] for d in d1)],
+                dst_ref=recv_d[t].at[n - 1],
+                send_sem=r_send.at[1],
+                recv_sem=r_recv.at[t, 1],
+                device_id=device(pos, core),
+                device_id_type=MESH,
+            ).start()
 
     def phase_a(u):
         ch, whose, piece = UNITS[u]
@@ -323,9 +345,14 @@
             total += recv_a[t][off - 1].astype(F32)
         acc_a[t][...] = total
         send_b[t][...] = total.astype(send_b[t].dtype)
-        launch(t, 1)
+        if t in DIRECT_TILES:
+            launch_direct(t)
+        else:
+            launch(t, 1)
 
     def phase_c(t):
+        if t in DIRECT_TILES:
+            return
         axis = order_of(t)[1]
         wait_for(recv_b[t], r_recv.at[t, 1])
         total = acc_a[t][pick(dims_of(t)[0], axis, me[axis])]
@@ -336,11 +363,20 @@
         launch(t, 2)
 
     def finish(t):
-        axis = order_of(t)[2]
-        wait_for(recv_c[t], r_recv.at[t, 2])
-        total = acc_b[t][pick(dims_of(t)[1], axis, me[axis])]
-        for off in (1, 2, 3):
-            total += recv_c[t][off - 1].astype(F32)
+        _, one, two = order_of(t)
+        d1, d2 = dims_of(t)
+        if t in DIRECT_TILES:
+            wait_for(recv_d[t], r_recv.at[t, 1])
+            at = dict(zip(d1, pick(d1, one, me[one])))
+            at.update(zip(d2, pick(d2, two, me[two])))
+            total = acc_a[t][tuple(at[d] for d in d1)]
+            for n in range(15):
+                total += recv_d[t][n].astype(F32)
+        else:
+            wait_for(recv_c[t], r_recv.at[t, 2])
+            total = acc_b[t][pick(d2, two, me[two])]
+            for off in (1, 2, 3):
+                total += recv_c[t][off - 1].astype(F32)
         ch, whose, piece = UNITS[t // 2]
         at = (M_CHUNKS[ch][0] + piece * QW) // 128 + t % 2
         out[:, tile(at, core if whose == 0 else 1 - core)] = total * (1.0 / 256.0)
@@ -377,8 +413,7 @@
         swap(n).wait_send()
     wait_for(mine, x_send)
     wait_for(send_a.at[pl.ds(0, NT * 3 // 8)], r_send.at[0])
-    wait_for(mx.at[pl.ds(0, 3), pl.ds(0, NT * 8)], r_send.at[1])
-    wait_for(mx.at[pl.ds(0, 3), pl.ds(0, NT * 2)], r_send.at[2])
+    wait_for(mx.at[pl.ds(0, 3), pl.ds(0, NT * 10)], r_send.at[1])
 
 
 def local(integrals, occupied, virtual, pair_mask, green_mask):
@@ -415,9 +450,10 @@
         *[vmem(s, F32) for s in d2],
         *[vmem(s, BF16) for s in d2],
         *[vmem((3, 16, 128), BF16) for _ in d2],
+        *[vmem((15, 16, 128), BF16) for _ in DIRECT_TILES],
         dma, dma, dma((4,)),
         dma((nh,)), dma((nh,)), dma((nm,)), dma((nm,)), dma((nm,)), dma((nm,)),
-        dma((3,)), dma((NT, 3)), dma((4,)),
+        dma((2,)), dma((NT, 3)), dma((4,)),
         pltpu.SemaphoreType.REGULAR((2,)),
     ]
     return pl.pallas_call(

time: 86.6 us -> 84.2 us (0.972)
  Pallas kernels: 84.5 us -> 82.4 us
    pallas_call x1, Pallas kernels: 84.5 us -> 82.4 us  [local(): pl.pallas_call(kernel, out_shape=jax.ShapeDtypeStruct((16, 2048), F32), i...]
where the time goes in v4:
time: 84.2 us; the launch traced here: 84 us
  Pallas kernels  82.4 us (98%)
  local copies, waits for them, and re-layouts  1.57 us (2%)
    pallas_call x1, Pallas kernels, local(): pl.pallas_call(kernel, out_shape=jax.ShapeDtypeStruct((16, 2048), F32), i...  82.4 us

profile of v4, /device:TPU:0, one launch (start us, length us, event | category | flops | bytes accessed | tf_op | source)
XLA Modules:
  0.0 84.0 jit_solution(15960982782242533362)
XLA Ops:
  0.0 82.4 %polarizability.1 = f32[16,2048]{1,0:T(8,128)} custom-call(bf16[2,256,2048]{2,1,0:T(8,128)(2,1)} %bitcast.1, bf16[256,256]{1,0:T(8,128)(2,1)} %refs_1_.1, bf16[256,256]{1,0:T(8,128)(2,1)} %refs_2_.1, s32[16,32]{1,0:T(8,128)} %refs_3_.1, s32[2,4,4]{2,1,0:T(4,128)} %refs_4_.1), custom_call_target="tpu_custom_call" | custom-call | tf_op jit(solution)/shard_map/polarizability/pallas_call | solution.py:459
  82.4 1.6 %copy.7 = f32[16,2048]{1,0:T(8,128)} copy(f32[16,2048]{1,0:T(8,128)} %polarizability.1) | data formatting | bytes 262144

commit v5 on v4

--- a/solution.py
+++ b/solution.py
@@ -229,11 +229,11 @@
         for start, at in pieces(first, width):
             to_chips(mx, msend[n], pl.ds(start, QW), pl.ds(at, QW))
 
+    make_h(0)
     pl.semaphore_wait(ready.at[0], 9)
     for off in (1, 2, 3):
         there = device(along("z", off), core)
         pl.semaphore_signal(ready.at[1], inc=1, device_id=there, device_id_type=MESH)
-    make_h(0)
     send_h(0, 0)
     make_h(1)
     pl.semaphore_wait(ready.at[1], 3)

time: 84.2 us -> 84.2 us (level)
  no operation moved by 1% of the time
where the time goes in v5:
time: 84.2 us; the launch traced here: 84 us
  Pallas kernels  82.5 us (98%)
  local copies, waits for them, and re-layouts  1.57 us (2%)
    pallas_call x1, Pallas kernels, local(): pl.pallas_call(kernel, out_shape=jax.ShapeDtypeStruct((16, 2048), F32), i...  82.5 us

profile of v5, /device:TPU:0, one launch (start us, length us, event | category | flops | bytes accessed | tf_op | source)
XLA Modules:
  0.0 84.0 jit_solution(1411626522250736778)
XLA Ops:
  0.0 82.5 %polarizability.1 = f32[16,2048]{1,0:T(8,128)} custom-call(bf16[2,256,2048]{2,1,0:T(8,128)(2,1)} %bitcast.1, bf16[256,256]{1,0:T(8,128)(2,1)} %refs_1_.1, bf16[256,256]{1,0:T(8,128)(2,1)} %refs_2_.1, s32[16,32]{1,0:T(8,128)} %refs_3_.1, s32[2,4,4]{2,1,0:T(4,128)} %refs_4_.1), custom_call_target="tpu_custom_call" | custom-call | tf_op jit(solution)/shard_map/polarizability/pallas_call | solution.py:459
  82.5 1.6 %copy.7 = f32[16,2048]{1,0:T(8,128)} copy(f32[16,2048]{1,0:T(8,128)} %polarizability.1) | data formatting | bytes 262144

commit v6 on v4

--- a/solution.py
+++ b/solution.py
@@ -12,7 +12,7 @@
 MESH = pl.DeviceIdType.MESH
 QW = 256
 H_CHUNKS = ((0, 256), (256, 256), (512, 512))
-M_CHUNKS = ((0, 256), (256, 256), (512, 512))
+M_CHUNKS = ((0, 512), (512, 512))
 UNITS = tuple(
     (ch, whose, piece) for ch, (_, w) in enumerate(M_CHUNKS) for whose in range(2) for piece in range(w // QW)
 )
@@ -56,7 +56,7 @@
     return d1, left_after(d1, order_of(t)[1])
 
 
-DIRECT = (6, 7)
+DIRECT = (4, 5, 6, 7)
 AHEAD = len(M_CHUNKS)
 PLAN = (("a", 0, 8), ("b", 0, 8), ("c", 0, 8), ("f", 0, 8))
 

time: 84.2 us -> 84.2 us (level)
  no operation moved by 1% of the time
where the time goes in v6:
time: 84.2 us; the launch traced here: 83.7 us
  Pallas kernels  82.1 us (98%)
  local copies, waits for them, and re-layouts  1.57 us (2%)
    pallas_call x1, Pallas kernels, local(): pl.pallas_call(kernel, out_shape=jax.ShapeDtypeStruct((16, 2048), F32), i...  82.1 us

profile of v6, /device:TPU:0, one launch (start us, length us, event | category | flops | bytes accessed | tf_op | source)
XLA Modules:
  0.0 83.7 jit_solution(1993135240618851951)
XLA Ops:
  0.0 82.1 %polarizability.1 = f32[16,2048]{1,0:T(8,128)} custom-call(bf16[2,256,2048]{2,1,0:T(8,128)(2,1)} %bitcast.1, bf16[256,256]{1,0:T(8,128)(2,1)} %refs_1_.1, bf16[256,256]{1,0:T(8,128)(2,1)} %refs_2_.1, s32[16,32]{1,0:T(8,128)} %refs_3_.1, s32[2,4,4]{2,1,0:T(4,128)} %refs_4_.1), custom_call_target="tpu_custom_call" | custom-call | tf_op jit(solution)/shard_map/polarizability/pallas_call | solution.py:459
  82.1 1.6 %copy.7 = f32[16,2048]{1,0:T(8,128)} copy(f32[16,2048]{1,0:T(8,128)} %polarizability.1) | data formatting | bytes 262144
